TPU v7x, 32 devices: a whole 2x2x4 slice. The times are simulated.
32 devices in a mesh: lat: 8 (over z, x), deg: 4 (over y, core).
Axes of the slice: x: 2, y: 2, z: 4, core: 2. Of those that a mesh axis runs over, the one named last changes fastest.
Arguments:
- eta_tl: float32 [64, 10752], P('lat'), may hold values from -6 to 6
- vel_tl: float32 [2, 64, 10752], P(None, 'lat'), may hold values from -6 to 6
- eta_adj: float32 [64, 10752], P('lat'), may hold values from -6 to 6
- vel_adj: float32 [2, 64, 10752], P(None, 'lat'), may hold values from -6 to 6
- depth: float32 [64, 10752], P('lat'), may hold values from 0.2 to 1
- drag: float32 [64, 10752], P('lat'), may hold values from 0.01 to 0.3
- ocean: int32 [64, 10752], P('lat'), may hold values 0 or 1
- basis: bfloat16 [1024, 64, 1024], P('lat', None, 'deg'), may hold values from -5 to 5
- love: float32 [1024], P('deg'), may hold values from 0.05 to 0.5
Outputs:
- eta_tl_out: float32 [64, 10752], P('lat')
- vel_tl_out: float32 [2, 64, 10752], P(None, 'lat')
- eta_adj_out: float32 [64, 10752], P('lat')
- vel_adj_out: float32 [2, 64, 10752], P(None, 'lat')
All inputs are finite; a program needn't handle non-finite values. No bound on the sum of `ocean` on one device may be relied on, other than what follows from the above.
Results may differ from a plain program's by a relative error of at most 0.02.
Values may be sent and summed in bfloat16 or wider, within the bound.
A program may use at most 320 MiB of HBM per device.

v0:
```python
import jax
import jax.numpy as jnp
from jax import lax
from jax.sharding import PartitionSpec as P

STEPS = 2
kappa_x = 0.3
kappa_y = 0.4


def as_sent(value):
    return jax.tree.map(lambda a: a.astype(jnp.bfloat16) if a.dtype == jnp.float32 else a, value)


def passed_along(value, axis, by):
    length = lax.axis_size(axis)
    pairs = [(i, i + by) for i in range(length) if 0 <= i + by < length]
    return lax.ppermute(value, axis, pairs)


def trig_table(orders, lon_count):
    lon_cells = jnp.arange(lon_count, dtype=jnp.int32)
    phase_index = lon_cells[:, None] * orders[None, :] % lon_count
    angles = phase_index.astype(jnp.float32) * (2.0 * jnp.pi / lon_count)
    return jnp.concatenate([jnp.cos(angles), jnp.sin(angles)], axis=1).astype(jnp.bfloat16)


def order_factor(orders):
    return jnp.where(orders == 0, 1.0, 2.0).astype(jnp.bfloat16)


def analyse(stacked, analysis_weight, table_now, order_count):
    row_count = stacked.shape[1]
    lon_count = stacked.shape[2]
    flat_rows = stacked.astype(jnp.bfloat16).reshape(2 * row_count, lon_count)
    spectra = lax.dot_general(
        table_now, flat_rows, (((0,), (1,)), ((), ())), preferred_element_type=jnp.float32
    )
    spectra = spectra.reshape(2, order_count, 2, row_count) * (1.0 / lon_count)
    return (spectra * analysis_weight[None, None, :, :]).astype(jnp.bfloat16)


def legendre(spectra, basis, love):
    coeffs = jnp.einsum("cmfi,mil->cmfl", spectra, basis, preferred_element_type=jnp.float32)
    scaled = (coeffs * love[None, None, None, :]).astype(jnp.bfloat16)
    return jnp.einsum("cmfl,mil->cmfi", scaled, basis, preferred_element_type=jnp.float32)


def synthesise(coeffs, factors, table_now, output_weight):
    order_count = coeffs.shape[1]
    row_count = coeffs.shape[3]
    scaled = (coeffs * factors[None, :, None, None]).reshape(2 * order_count, 2 * row_count)
    grid_out = lax.dot_general(
        scaled, table_now, (((0,), (1,)), ((), ())), preferred_element_type=jnp.float32
    )
    return grid_out.reshape(2, row_count, -1) * output_weight[:, :, None]


def from_north(edge_row):
    return passed_along(as_sent(edge_row), "lat", -1).astype(edge_row.dtype)


def from_south(edge_row):
    return passed_along(as_sent(edge_row), "lat", 1).astype(edge_row.dtype)


def on_device(eta_tl, vel_tl, eta_adj, vel_adj, depth, drag, ocean, basis, love):
    row_count = eta_tl.shape[0]
    lon_count = eta_tl.shape[1]
    lat_count = lax.axis_size("lat")
    total_rows = row_count * lat_count
    first_row = lax.axis_index("lat") * row_count
    indices = first_row + jnp.arange(row_count, dtype=jnp.int32)
    latitude = (indices.astype(jnp.float32) + 0.5) * (jnp.pi / total_rows) - 0.5 * jnp.pi
    cosine = jnp.cos(latitude)
    quad_weight = jnp.pi / total_rows * cosine
    east_factor = (kappa_x / (0.5 + 0.5 * cosine))[:, None]
    wet_mask = ocean.astype(jnp.float32)
    north_depth, north_wet = (
        passed_along(depth[:1].astype(jnp.bfloat16), "lat", -1).astype(jnp.float32),
        passed_along(wet_mask[:1].astype(jnp.bfloat16), "lat", -1).astype(jnp.float32),
    )
    depth_up = jnp.concatenate([depth[1:], north_depth], 0)
    wet_up = jnp.concatenate([wet_mask[1:], north_wet], 0)
    mask_u = wet_mask * jnp.roll(wet_mask, -1, 1)
    mask_v = wet_mask * wet_up
    depth_u = 0.5 * (depth + jnp.roll(depth, -1, 1))
    depth_v = 0.5 * (depth + depth_up)
    retain = 1.0 - drag
    ones_weight = jnp.ones_like(quad_weight)
    analysis_weight = jnp.stack([quad_weight, ones_weight])
    output_weight = jnp.stack([ones_weight, quad_weight])
    owned_count = basis.shape[0]
    order_total = owned_count * lat_count
    full_orders = jnp.arange(order_total, dtype=jnp.int32)
    full_table = trig_table(full_orders, lon_count)
    full_factor = order_factor(full_orders)
    state_eta, state_vel = (eta_tl, vel_tl)
    back_eta, back_vel = (eta_adj, vel_adj)
    for step_index in range(STEPS):
        flux_east = east_factor * wet_mask * back_eta
        flux_north = kappa_y * wet_mask * back_eta
        north_up = jnp.concatenate([flux_north[1:], from_north(flux_north[:1])], 0)
        p_term = mask_u * (back_vel[0] + depth_u * (jnp.roll(flux_east, -1, 1) - flux_east))
        q_term = mask_v * (back_vel[1] + depth_v * (north_up - flux_north))
        q_down = jnp.concatenate([from_south(q_term[-1:]), q_term[:-1]], 0)
        flux_p = east_factor * p_term
        psi_bar = flux_p - jnp.roll(flux_p, 1, 1) + kappa_y * (q_term - q_down)
        spectra = analyse(jnp.stack([state_eta, psi_bar]), analysis_weight, full_table, order_total)
        owned_rows = lax.all_to_all(spectra, "lat", split_axis=1, concat_axis=3, tiled=True)
        partial_value = legendre(owned_rows, basis, love)
        total_sum = lax.psum(partial_value.astype(jnp.bfloat16), "deg")
        banded = lax.all_to_all(total_sum, "lat", split_axis=3, concat_axis=1, tiled=True)
        loads = synthesise(banded, full_factor, full_table, output_weight)
        psi_now = state_eta - loads[0]
        psi_up = jnp.concatenate([psi_now[1:], from_north(psi_now[:1])], 0)
        new_u = mask_u * (
            retain * state_vel[0] - east_factor * (jnp.roll(psi_now, -1, 1) - psi_now)
        )
        new_v = mask_v * (retain * state_vel[1] - kappa_y * (psi_up - psi_now))
        flux_x = depth_u * new_u
        flux_y = depth_v * new_v
        flux_down = jnp.concatenate([from_south(flux_y[-1:]), flux_y[:-1]], 0)
        state_eta = state_eta - wet_mask * (
            east_factor * (flux_x - jnp.roll(flux_x, 1, 1)) + kappa_y * (flux_y - flux_down)
        )
        state_vel = jnp.stack([new_u, new_v])
        back_eta = back_eta + psi_bar - loads[1]
        back_vel = jnp.stack([retain * p_term, retain * q_term])
    return (state_eta, state_vel, back_eta, back_vel)


def solution(mesh):
    in_specs = (
        P("lat", None),
        P(None, "lat", None),
        P("lat", None),
        P(None, "lat", None),
        P("lat", None),
        P("lat", None),
        P("lat", None),
        P("lat", None, "deg"),
        P("deg"),
    )
    out_specs = (P("lat", None), P(None, "lat", None), P("lat", None), P(None, "lat", None))
    return jax.shard_map(
        on_device, mesh=mesh, in_specs=in_specs, out_specs=out_specs, check_vma=False
    )
```

profile of v0, /device:TPU:0, one launch (start us, length us, event | category | flops | bytes accessed | tf_op | source)
XLA Modules:
  0.0 552.0 jit_solution(11705418563088993422)
XLA Ops:
  7.3 1.2 multiply_multiply_fusion.3
  8.5 1.3 collective-permute-start.2
  9.8 1.0 slice.281
  10.8 1.3 collective-permute-start.1
  12.1 1.0 convert_element_type.110
  13.2 1.3 collective-permute-start
  14.5 187.3 %sine_convert_fusion = (bf16[10752,1024]{1,0:T(8,128)(2,1)}, bf16[10752,1024]{1,0:T(8,128)(2,1)}) fusion(), kind=kLoop, calls=%fused_computation.8 | loop fusion | flops 121110528 | bytes 44040192 | tf_op jit(solution)/shard_map/convert.19
  201.8 0.7 convert_bitcast_fusion.3
  202.5 29.5 %fusion.9 = bf16[2048,10752]{0,1:T(8,128)(2,1)} fusion(bf16[10752,1024]{1,0:T(8,128)(2,1)} %get-tuple-element.48, bf16[10752,1024]{1,0:T(8,128)(2,1)} %get-tuple-element.49), kind=kLoop, calls=%fused_computation.14 | loop fusion | flops 88080384 | bytes 88080384 | tf_op jit(solution)/shard_map/dot_general | solution.py:36
  232.1 0.1 slice.208
  232.2 0.1 slice.206
  232.4 0.1 slice.158
  232.9 2.4 broadcast_multiply_fusion.1
  235.3 6.7 %collective-permute-start.3 = (bf16[1,10752]{1,0:T(2,128)(2,1)S(1)}, bf16[1,10752]{1,0:T(2,128)(2,1)S(1)}, u32[]{:S(2)}, u32[]{:S(2)}) collective-permute-start(bf16[1,10752]{1,0:T(2,128)(2,1)S(1)} %slice.279), channel_id=1, source_target_pairs={{0,4},{4,8},{8,12},{12,16},{16,20},{20,24},{24,28},{1,5},{5,9},{9,... | collective-permute-start | bytes 64520 | tf_op jit(solution)/shard_map/ppermute | solution.py:18
  242.1 56.8 %copy.41 = bf16[2048,10752]{1,0:T(8,128)(2,1)} copy(bf16[2048,10752]{0,1:T(8,128)(2,1)} %fusion.9) | data formatting | bytes 88080384 | tf_op jit(solution)/shard_map/dot_general | solution.py:36
  299.0 0.9 convert_bitcast_fusion.2
  299.9 19.5 %fusion.66 = bf16[2,1024,2,8]{1,3,2,0:T(8,128)(2,1)S(1)} fusion(bf16[2,1024,10752,1]{2,1,3,0:T(8,128)(2,1)} %bitcast.190, bf16[1,8,10752]{2,1,0:T(8,128)(2,1)S(1)} %get-tuple-element.22, bf16[1,8,10752]{2,1,0:T(8,128)(2,1)S(1)} %copy-done.10, f32[2,8]{1,0:T(2,128)S(1)} %get-tuple-element.46), kind=kOutput, calls=%fused_computation.37 | convolution fusion | flops 705396736 | bytes 44449856 | tf_op jit(solution)/shard_map/dot_general | solution.py:36
  319.3 0.7 copy.42
  320.1 1.1 reshape.79
  321.2 14.8 %all_to_all.72 = bf16[8,2,2048]{2,1,0:T(2,128)(2,1)S(1)} all-to-all(bf16[8,2,2048]{2,1,0:T(2,128)(2,1)S(1)} %reshape.79), channel_id=1, replica_groups=mesh['lat'=8,'deg'=4] {'lat'}, dimensions={0} | all-to-all | bytes 131072 | tf_op jit(solution)/shard_map/all_to_all | solution.py:110
  336.0 1.2 reshape.80
  337.2 1.3 copy.59
  338.6 6.0 %fusion.61 = bf16[2,128,2,64]{3,2,0,1:T(2,128)(2,1)} fusion(bf16[128,64,256]{2,1,0:T(8,128)(2,1)} %param.16, bf16[2,128,2,64]{3,2,0,1:T(2,128)(2,1)S(1)} %copy.45, f32[256]{0:T(256)S(1)} %copy-done.11), kind=kOutput, calls=%fused_computation.34 | convolution fusion | flops 33849344 | bytes 4326400 | tf_op jit(solution)/shard_map/cmfl,mil->cmfi/dot_general | solution.py:46
  344.7 29.1 %all-reduce.5.cloned.1.call-done = bf16[2,128,2,64]{3,2,0,1:T(2,128)(2,1)} async-done(((bf16[2,128,2,64]{3,2,0,1:T(2,128)(2,1)}), bf16[2,128,2,64]{3,2,0,1:T(2,128)(2,1)}) %all-reduce.5.cloned.1.call-update) | async-done | bytes 65552 | tf_op jit(solution)/shard_map/psum | solution.py:112
  373.8 1.7 copy.46
  375.5 5.5 all-to-all-start.1
  381.1 6.8 %all-to-all-done.1 = bf16[2,128,2,64]{1,2,0,3:T(2,128)(2,1)S(1)} async-done(((bf16[2,128,2,64]{1,2,0,3:T(2,128)(2,1)}), bf16[2,128,2,64]{1,2,0,3:T(2,128)(2,1)S(1)}, u32[]{:S(2)}, u32[]{:S(2)}) %all-to-all-start.1) | async-done | bytes 65568 | tf_op jit(solution)/shard_map/all_to_all | solution.py:113
  388.0 18.4 %fusion.10 = f32[2,8,10752]{2,1,0:T(8,128)} fusion(bf16[10752,1024]{1,0:T(8,128)(2,1)} %get-tuple-element.48, bf16[10752,1024]{1,0:T(8,128)(2,1)} %get-tuple-element.49, f32[2,8]{1,0:T(2,128)S(1)} %get-tuple-element.47, bf16[2048,16]{0,1:T(8,128)(2,1)S(1)} %all_to_all.59, bf16[2048]{0:T(1024)(128)(2,1)S(1)} %bitcast.210), kind=kOutput, calls=%fused_computation.15 | convolution fusion | flops 792928256 | bytes 44798016 | tf_op jit(solution)/shard_map/dot_general | solution.py:53
  406.4 1.4 multiply_multiply_fusion
  407.8 1.3 collective-permute-start.4
  409.2 1.3 collective-permute-start.6
  410.5 0.1 slice.220
  410.7 3.0 collective-permute-done.4
  413.8 1.9 collective-permute-done.6
  415.8 2.4 fusion.139
  418.2 4.8 collective-permute-start.5
  423.2 2.3 collective-permute-start.7
  425.5 0.3 convert_bitcast_fusion.1
  425.8 0.1 slice.229
  425.9 1.8 multiply_bitcast_fusion.1
  428.0 0.2 convert_bitcast_fusion
  428.2 19.5 %fusion.67 = bf16[2,1024,2,8]{1,3,2,0:T(8,128)(2,1)S(1)} fusion(bf16[2,1024,10752,1]{2,1,3,0:T(8,128)(2,1)} %bitcast.191, bf16[1,8,10752]{2,1,0:T(8,128)(2,1)S(1)} %get-tuple-element.14, bf16[1,8,10752]{2,1,0:T(8,128)(2,1)S(1)} %get-tuple-element.12, f32[2,8]{1,0:T(2,128)S(1)} %get-tuple-element.46), kind=kOutput, calls=%fused_computation.38 | convolution fusion | flops 705396736 | bytes 44449856 | tf_op jit(solution)/shard_map/dot_general | solution.py:36
  447.7 0.7 copy.49
  448.4 1.1 reshape.81
  449.5 10.5 %all_to_all.73 = bf16[8,2,2048]{2,1,0:T(2,128)(2,1)S(1)} all-to-all(bf16[8,2,2048]{2,1,0:T(2,128)(2,1)S(1)} %reshape.81), channel_id=1, replica_groups=mesh['lat'=8,'deg'=4] {'lat'}, dimensions={0} | all-to-all | bytes 131072 | tf_op jit(solution)/shard_map/all_to_all | solution.py:110
  460.0 1.2 reshape.82
  461.2 1.3 copy.61
  462.5 0.8 copy.52
  463.3 6.1 %fusion.56 = bf16[2,128,2,64]{3,2,0,1:T(2,128)(2,1)} fusion(bf16[128,64,256]{2,1,0:T(8,128)(2,1)} %param.16, bf16[2,128,2,64]{3,2,0,1:T(2,128)(2,1)} %copy.52, f32[256]{0:T(256)S(1)} %copy-done.11), kind=kOutput, calls=%fused_computation.33 | convolution fusion | flops 33849344 | bytes 4326400 | tf_op jit(solution)/shard_map/cmfl,mil->cmfi/dot_general | solution.py:46
  469.4 28.1 %all-reduce.7.cloned.1.call-done = bf16[2,128,2,64]{3,2,0,1:T(2,128)(2,1)} async-done(((bf16[2,128,2,64]{3,2,0,1:T(2,128)(2,1)}), bf16[2,128,2,64]{3,2,0,1:T(2,128)(2,1)}) %all-reduce.7.cloned.1.call-update) | async-done | bytes 65552 | tf_op jit(solution)/shard_map/psum | solution.py:112
  497.6 1.0 copy.53
  498.6 12.2 %all_to_all.74 = bf16[2,128,2,64]{1,2,0,3:T(2,128)(2,1)S(1)} all-to-all(bf16[2,128,2,64]{1,2,0,3:T(2,128)(2,1)S(1)} %copy.53), channel_id=1, replica_groups=mesh['lat'=8,'deg'=4] {'lat'}, dimensions={3} | all-to-all | bytes 131072 | tf_op jit(solution)/shard_map/all_to_all | solution.py:113
  510.9 0.7 all_to_all.67
  511.5 18.4 %fusion.13 = f32[2,8,10752]{2,1,0:T(8,128)} fusion(bf16[10752,1024]{1,0:T(8,128)(2,1)} %get-tuple-element.48, bf16[10752,1024]{1,0:T(8,128)(2,1)} %get-tuple-element.49, f32[2,8]{1,0:T(2,128)S(1)} %get-tuple-element.47, bf16[2048,16]{0,1:T(8,128)(2,1)} %all_to_all.67, bf16[2048]{0:T(1024)(128)(2,1)S(1)} %bitcast.211), kind=kOutput, calls=%fused_computation.16 | convolution fusion | flops 792928256 | bytes 44798016 | tf_op jit(solution)/shard_map/dot_general | solution.py:53
  529.9 1.9 fusion.68
  531.9 1.3 collective-permute-start.8
  533.2 1.9 pad_maximum_fusion.4
  535.1 0.1 slice.238
  535.2 2.5 collective-permute-done.8
  537.8 1.4 fusion.130
  539.3 3.2 collective-permute-start.9
  542.5 0.9 pad_maximum_fusion.3
  543.4 0.7 collective-permute-done.9
  544.2 0.9 fusion.111
  (83 shorter events, 1.8 us)
Async XLA Ops:
  7.2 194.6 %copy-start.2 = (f32[8,10752]{1,0:T(8,128)S(1)}, f32[8,10752]{1,0:T(8,128)}, u32[]{:S(2)}) copy-start(f32[8,10752]{1,0:T(8,128)} %param.9) | copy-start | bytes 1032196
  7.2 366.7 %all-reduce.5.cloned.1.call-start = ((), (), s32[]{:S(2)}) async-start(), calls=%async_computation.4 | async-start | bytes 262144 | tf_op jit(solution)/shard_map/psum | solution.py:112
  8.5 224.2 %collective-permute-start.2 = (bf16[1,10752]{1,0:T(2,128)(2,1)S(1)}, bf16[1,10752]{1,0:T(2,128)(2,1)S(1)}, u32[]{:S(2)}, u32[]{:S(2)}) collective-permute-start(bf16[1,10752]{1,0:T(2,128)(2,1)S(1)} %slice.280), channel_id=1, source_target_pairs={{4,0},{8,4},{12,8},{16,12},{20,16},{24,20},{28,24},{5,1},{9,5},{13... | collective-permute-start | bytes 64520 | tf_op jit(solution)/shard_map/ppermute | solution.py:18
  10.8 221.9 %collective-permute-start.1 = (bf16[1,10752]{1,0:T(2,128)(2,1)S(1)}, bf16[1,10752]{1,0:T(2,128)(2,1)S(1)}, u32[]{:S(2)}, u32[]{:S(2)}) collective-permute-start(bf16[1,10752]{1,0:T(2,128)(2,1)S(1)} %slice.281), channel_id=1, source_target_pairs={{4,0},{8,4},{12,8},{16,12},{20,16},{24,20},{28,24},{5,1},{9,5},{13... | collective-permute-start | bytes 64520 | tf_op jit(solution)/shard_map/ppermute | solution.py:18
  13.2 219.7 %collective-permute-start = (bf16[1,10752]{1,0:T(2,128)(2,1)S(1)}, bf16[1,10752]{1,0:T(2,128)(2,1)S(1)}, u32[]{:S(2)}, u32[]{:S(2)}) collective-permute-start(bf16[1,10752]{1,0:T(2,128)(2,1)S(1)} %slice.282), channel_id=1, source_target_pairs={{4,0},{8,4},{12,8},{16,12},{20,16},{24,20},{28,24},{5,1},{9,5},{13... | collective-permute-start | bytes 64520 | tf_op jit(solution)/shard_map/ppermute | solution.py:18
  202.5 29.9 %copy-start.1 = (f32[8,10752]{1,0:T(8,128)S(1)}, f32[8,10752]{1,0:T(8,128)}, u32[]{:S(2)}) copy-start(f32[8,10752]{1,0:T(8,128)} %param.13) | copy-start | bytes 1032196
  202.5 30.4 %copy-start = (s32[8,10752]{1,0:T(8,128)S(1)}, s32[8,10752]{1,0:T(8,128)}, u32[]{:S(2)}) copy-start(s32[8,10752]{1,0:T(8,128)} %param.15) | copy-start | bytes 1032196
  202.5 30.4 %slice-start = ((f32[8,10752]{1,0:T(8,128)}), f32[8,1]{1,0:T(8,128)S(1)}, s32[]{:S(2)}) async-start(f32[8,10752]{1,0:T(8,128)} %param.13), calls=%async_computation.6 | async-start | bytes 8192 | tf_op jit(solution)/shard_map/jit(_roll_static)/slice | solution.py:87
  235.2 180.5 %copy-start.5 = (f32[8,10752]{1,0:T(8,128)}, f32[8,10752]{1,0:T(8,128)S(1)}, u32[]{:S(2)}) copy-start(f32[8,10752]{1,0:T(8,128)S(1)} %get-tuple-element.34) | copy-start | bytes 1032196
  235.3 63.6 %collective-permute-start.3 = (bf16[1,10752]{1,0:T(2,128)(2,1)S(1)}, bf16[1,10752]{1,0:T(2,128)(2,1)S(1)}, u32[]{:S(2)}, u32[]{:S(2)}) collective-permute-start(bf16[1,10752]{1,0:T(2,128)(2,1)S(1)} %slice.279), channel_id=1, source_target_pairs={{0,4},{4,8},{8,12},{12,16},{16,20},{20,24},{24,28},{1,5},{5,9},{9,... | collective-permute-start | bytes 64520 | tf_op jit(solution)/shard_map/ppermute | solution.py:18
  242.0 57.8 %copy-start.10 = (bf16[1,8,10752]{2,1,0:T(8,128)(2,1)S(1)}, bf16[1,8,10752]{2,1,0:T(8,128)(2,1)}, u32[]{:S(2)}) copy-start(bf16[1,8,10752]{2,1,0:T(8,128)(2,1)} %convert_bitcast_fusion.3) | copy-start | bytes 516100
  298.8 39.8 %copy-start.11 = (f32[256]{0:T(256)S(1)}, f32[256]{0:T(256)}, u32[]{:S(2)}) copy-start(f32[256]{0:T(256)} %param.17) | copy-start | bytes 3076
  338.6 77.2 %copy-start.3 = (f32[8,10752]{1,0:T(8,128)S(1)}, f32[8,10752]{1,0:T(8,128)}, u32[]{:S(2)}) copy-start(f32[8,10752]{1,0:T(8,128)} %param.14) | copy-start | bytes 1032196
  338.6 77.2 %copy-start.7 = (f32[8,10752]{1,0:T(8,128)S(1)}, f32[8,10752]{1,0:T(8,128)}, u32[]{:S(2)}) copy-start(f32[8,10752]{1,0:T(8,128)} %get-tuple-element.35) | copy-start | bytes 1032196
  375.5 12.4 %all-to-all-start.1 = ((bf16[2,128,2,64]{1,2,0,3:T(2,128)(2,1)}), bf16[2,128,2,64]{1,2,0,3:T(2,128)(2,1)S(1)}, u32[]{:S(2)}, u32[]{:S(2)}) async-start(bf16[2,128,2,64]{1,2,0,3:T(2,128)(2,1)} %copy.46), calls=%async_computation.1 | async-start | bytes 131072 | tf_op jit(solution)/shard_map/all_to_all | solution.py:113
  381.0 116.6 %all-reduce.7.cloned.1.call-start = ((), (), s32[]{:S(2)}) async-start(), calls=%async_computation.5 | async-start | bytes 262144 | tf_op jit(solution)/shard_map/psum | solution.py:112
  407.8 5.9 %collective-permute-start.4 = (bf16[1,10752]{1,0:T(2,128)(2,1)S(1)}, bf16[1,10752]{1,0:T(2,128)(2,1)S(1)}, u32[]{:S(2)}, u32[]{:S(2)}) collective-permute-start(bf16[1,10752]{1,0:T(2,128)(2,1)S(1)} %slice.278), channel_id=1, source_target_pairs={{4,0},{8,4},{12,8},{16,12},{20,16},{24,20},{28,24},{5,1},{9,5},{13... | collective-permute-start | bytes 64520 | tf_op jit(solution)/shard_map/ppermute | solution.py:18
  409.2 6.5 %collective-permute-start.6 = (bf16[1,10752]{1,0:T(2,128)(2,1)S(1)}, bf16[1,10752]{1,0:T(2,128)(2,1)S(1)}, u32[]{:S(2)}, u32[]{:S(2)}) collective-permute-start(bf16[1,10752]{1,0:T(2,128)(2,1)S(1)} %slice.276), channel_id=1, source_target_pairs={{4,0},{8,4},{12,8},{16,12},{20,16},{24,20},{28,24},{5,1},{9,5},{13... | collective-permute-start | bytes 64520 | tf_op jit(solution)/shard_map/ppermute | solution.py:18
  418.2 7.3 %collective-permute-start.5 = (bf16[1,10752]{1,0:T(2,128)(2,1)S(1)}, bf16[1,10752]{1,0:T(2,128)(2,1)S(1)}, u32[]{:S(2)}, u32[]{:S(2)}) collective-permute-start(bf16[1,10752]{1,0:T(2,128)(2,1)S(1)} %slice.277), channel_id=1, source_target_pairs={{0,4},{4,8},{8,12},{12,16},{16,20},{20,24},{24,28},{1,5},{5,9},{9,... | collective-permute-start | bytes 64520 | tf_op jit(solution)/shard_map/ppermute | solution.py:18
  423.2 4.8 collective-permute-start.7
  460.0 73.2 %copy-start.9 = (f32[1,8,10752]{2,1,0:T(8,128)S(1)}, f32[1,8,10752]{2,1,0:T(8,128)}, u32[]{:S(2)}) copy-start(f32[1,8,10752]{2,1,0:T(8,128)} %get-tuple-element.4) | copy-start | bytes 1032196
  463.3 74.5 %copy-start.4 = (f32[8,10752]{1,0:T(8,128)S(1)}, f32[8,10752]{1,0:T(8,128)}, u32[]{:S(2)}) copy-start(f32[8,10752]{1,0:T(8,128)} %param.14) | copy-start | bytes 1032196
  463.3 74.5 %copy-start.6 = (f32[8,10752]{1,0:T(8,128)S(1)}, f32[8,10752]{1,0:T(8,128)}, u32[]{:S(2)}) copy-start(f32[8,10752]{1,0:T(8,128)} %copy-done.5) | copy-start | bytes 1032196
  463.3 74.5 %copy-start.8 = (f32[8,10752]{1,0:T(8,128)S(1)}, f32[8,10752]{1,0:T(8,128)}, u32[]{:S(2)}) copy-start(f32[8,10752]{1,0:T(8,128)} %get-tuple-element.35) | copy-start | bytes 1032196
  531.9 5.9 %collective-permute-start.8 = (bf16[1,10752]{1,0:T(2,128)(2,1)S(1)}, bf16[1,10752]{1,0:T(2,128)(2,1)S(1)}, u32[]{:S(2)}, u32[]{:S(2)}) collective-permute-start(bf16[1,10752]{1,0:T(2,128)(2,1)S(1)} %slice.274), channel_id=1, source_target_pairs={{4,0},{8,4},{12,8},{16,12},{20,16},{24,20},{28,24},{5,1},{9,5},{13... | collective-permute-start | bytes 64520 | tf_op jit(solution)/shard_map/ppermute | solution.py:18
  539.3 4.9 collective-permute-start.9
Sparse Core Ops, SparseCore 0:
  344.8 28.9 all-reduce.4
  469.6 27.9 all-reduce.6
where the time goes:
time: 554 us; the launch traced here: 552 us
  other arithmetic  237 us (43%)
  matrix products  88 us (16%)
  local copies, waits for them, and re-layouts  72.5 us (13%)
  waiting for transfers between devices  72.3 us (13%)
  blocking collectives  37.5 us (7%)
  starting transfers between devices  30.4 us (5%)
  between operations  14.7 us (3%)
    another operation x1, other arithmetic  187 us
    psum x2, waiting for transfers between devices, on_device(): total_sum = lax.psum(partial_value.astype(jnp.bfloat16), 'deg')  57.2 us
    dot_general x1, local copies, waits for them, and re-layouts, analyse(): lax.dot_general(table_now, flat_rows, (((0,), (1,)), ((), ())), preferred...  56.8 us
    dot_general x2, matrix products, analyse(): lax.dot_general(table_now, flat_rows, (((0,), (1,)), ((), ())), preferred...  39 us
    dot_general x2, matrix products, synthesise(): lax.dot_general(scaled, table_now, (((0,), (1,)), ((), ())), preferred_el...  36.8 us
    dot_general x1, other arithmetic, analyse(): lax.dot_general(table_now, flat_rows, (((0,), (1,)), ((), ())), preferred...  29.5 us
    all_to_all x2, blocking collectives, on_device(): lax.all_to_all(spectra, 'lat', split_axis=1, concat_axis=3, tiled=True)  25.3 us
    ppermute x10, starting transfers between devices, passed_along(): return lax.ppermute(value, axis, pairs)  24.8 us
  transfers between devices with their start and end apart: 13, of which 7 were waited for; matrix products, arithmetic and copies ran while one was open for 51% of the time, Pallas kernels for 0%

commit v1 on v0

--- a/solution.py
+++ b/solution.py
@@ -110,7 +110,19 @@
         owned_rows = lax.all_to_all(spectra, "lat", split_axis=1, concat_axis=3, tiled=True)
         partial_value = legendre(owned_rows, basis, love)
         total_sum = lax.psum(partial_value.astype(jnp.bfloat16), "deg")
-        banded = lax.all_to_all(total_sum, "lat", split_axis=3, concat_axis=1, tiled=True)
+        ways, here = (lax.axis_size("lat"), lax.axis_index("lat"))
+        width = total_sum.shape[3] // ways
+        shape = list(total_sum.shape)
+        shape[3] = width
+        height = shape[1]
+        shape[1] = height * ways
+        full = jnp.zeros(shape, total_sum.dtype)
+        for mask in range(ways):
+            part = lax.dynamic_slice_in_dim(total_sum, (here ^ mask) * width, width, axis=3)
+            if mask:
+                part = lax.ppermute(part, "lat", [(d, d ^ mask) for d in range(ways)])
+            full = lax.dynamic_update_slice_in_dim(full, part, (here ^ mask) * height, axis=1)
+        banded = full
         loads = synthesise(banded, full_factor, full_table, output_weight)
         psi_now = state_eta - loads[0]
         psi_up = jnp.concatenate([psi_now[1:], from_north(psi_now[:1])], 0)

time: 554 us -> 591 us (1.067)
  starting transfers between devices: 30.4 us -> 47.7 us
  local copies, waits for them, and re-layouts: 72.5 us -> 87.3 us
  waiting for transfers between devices: 72.3 us -> 85.8 us
  blocking collectives: 37.5 us -> 27.4 us
    ppermute x0 -> x14, starting transfers between devices: none -> 22.5 us  [on_device(): part = lax.ppermute(part, 'lat', [(d, d ^ mask) for d in range(ways)])]
    ppermute x0 -> x14, waiting for transfers between devices: none -> 20.2 us  [on_device(): part = lax.ppermute(part, 'lat', [(d, d ^ mask) for d in range(ways)])]
    ppermute x0 -> x14, local copies, waits for them, and re-layouts: none -> 13.9 us  [on_device(): part = lax.ppermute(part, 'lat', [(d, d ^ mask) for d in range(ways)])]
    all_to_all x1 -> x0, blocking collectives: 12.2 us -> none  [on_device(): lax.all_to_all(total_sum, 'lat', split_axis=3, concat_axis=1, tiled=True)]
    dynamic_slice x0 -> x4, local copies, waits for them, and re-layouts: none -> 8.45 us  [on_device(): lax.dynamic_slice_in_dim(total_sum, (here ^ mask) * width, width, axis=3)]
    all_to_all x1 -> x0, waiting for transfers between devices: 6.84 us -> none  [on_device(): lax.all_to_all(total_sum, 'lat', split_axis=3, concat_axis=1, tiled=True)]
  transfers between devices with their start and end apart: 13 -> 26, of which waited for: 7 -> 10; matrix products, arithmetic and copies ran while one was open for 51% -> 49% of each run, Pallas kernels for 0% -> 0%
where the time goes in v1:
time: 591 us; the launch traced here: 588 us
  other arithmetic  237 us (40%)
  matrix products  87.8 us (15%)
  local copies, waits for them, and re-layouts  87.3 us (15%)
  waiting for transfers between devices  85.8 us (15%)
  starting transfers between devices  47.7 us (8%)
  blocking collectives  27.4 us (5%)
  between operations  15 us (3%)
    another operation x1, other arithmetic  187 us
    psum x2, waiting for transfers between devices, on_device(): total_sum = lax.psum(partial_value.astype(jnp.bfloat16), 'deg')  57.4 us
    dot_general x1, local copies, waits for them, and re-layouts, analyse(): lax.dot_general(table_now, flat_rows, (((0,), (1,)), ((), ())), preferred...  51.3 us
    dot_general x2, matrix products, analyse(): lax.dot_general(table_now, flat_rows, (((0,), (1,)), ((), ())), preferred...  38.8 us
    dot_general x2, matrix products, synthesise(): lax.dot_general(scaled, table_now, (((0,), (1,)), ((), ())), preferred_el...  36.8 us
    dot_general x1, other arithmetic, analyse(): lax.dot_general(table_now, flat_rows, (((0,), (1,)), ((), ())), preferred...  29.5 us
    all_to_all x2, blocking collectives, on_device(): lax.all_to_all(spectra, 'lat', split_axis=1, concat_axis=3, tiled=True)  27.4 us
    ppermute x10, starting transfers between devices, passed_along(): return lax.ppermute(value, axis, pairs)  25.1 us
  transfers between devices with their start and end apart: 26, of which 10 were waited for; matrix products, arithmetic and copies ran while one was open for 49% of the time, Pallas kernels for 0%

profile of v1, /device:TPU:0, one launch (start us, length us, event | category | flops | bytes accessed | tf_op | source)
XLA Modules:
  0.0 587.8 jit_solution(3181989039960776486)
XLA Ops:
  7.3 1.2 multiply_multiply_fusion.3
  8.5 1.3 collective-permute-start.2
  9.8 1.0 slice.281
  10.8 1.3 collective-permute-start.1
  12.1 1.0 convert_element_type.110
  13.2 1.3 collective-permute-start
  14.5 187.3 %sine_convert_fusion = (bf16[10752,1024]{1,0:T(8,128)(2,1)}, bf16[10752,1024]{1,0:T(8,128)(2,1)}) fusion(), kind=kLoop, calls=%fused_computation.8 | loop fusion | flops 121110528 | bytes 44040192 | tf_op jit(solution)/shard_map/convert.19
  202.5 29.5 %fusion.9 = bf16[2048,10752]{0,1:T(8,128)(2,1)} fusion(bf16[10752,1024]{1,0:T(8,128)(2,1)} %get-tuple-element.64, bf16[10752,1024]{1,0:T(8,128)(2,1)} %get-tuple-element.65), kind=kLoop, calls=%fused_computation.14 | loop fusion | flops 88080384 | bytes 88080384 | tf_op jit(solution)/shard_map/dot_general | solution.py:36
  232.8 2.4 broadcast_multiply_fusion.1
  235.2 6.7 %collective-permute-start.3 = (bf16[1,10752]{1,0:T(2,128)(2,1)S(1)}, bf16[1,10752]{1,0:T(2,128)(2,1)S(1)}, u32[]{:S(2)}, u32[]{:S(2)}) collective-permute-start(bf16[1,10752]{1,0:T(2,128)(2,1)S(1)} %slice.279), channel_id=1, source_target_pairs={{0,4},{4,8},{8,12},{12,16},{16,20},{20,24},{24,28},{1,5},{5,9},{9,... | collective-permute-start | bytes 64520 | tf_op jit(solution)/shard_map/ppermute | solution.py:18
  242.0 51.3 %copy.73 = bf16[2048,10752]{1,0:T(8,128)(2,1)} copy(bf16[2048,10752]{0,1:T(8,128)(2,1)} %fusion.9) | data formatting | bytes 88080384 | tf_op jit(solution)/shard_map/dot_general | solution.py:36
  294.3 19.4 %fusion.66 = bf16[2,1024,2,8]{1,3,2,0:T(8,128)(2,1)S(1)} fusion(bf16[2,1024,10752,1]{2,1,3,0:T(8,128)(2,1)} %bitcast.179, bf16[1,8,10752]{2,1,0:T(8,128)(2,1)S(1)} %get-tuple-element.22, bf16[1,8,10752]{2,1,0:T(8,128)(2,1)S(1)} %copy-done.10, f32[2,8]{1,0:T(2,128)S(1)} %get-tuple-element.62), kind=kOutput, calls=%fused_computation.37 | convolution fusion | flops 705396736 | bytes 44449856 | tf_op jit(solution)/shard_map/dot_general | solution.py:36
  314.5 1.1 reshape.81
  315.5 14.8 %all_to_all.36 = bf16[8,2,2048]{2,1,0:T(2,128)(2,1)S(1)} all-to-all(bf16[8,2,2048]{2,1,0:T(2,128)(2,1)S(1)} %reshape.81), channel_id=1, replica_groups=mesh['lat'=8,'deg'=4] {'lat'}, dimensions={0} | all-to-all | bytes 131072 | tf_op jit(solution)/shard_map/all_to_all | solution.py:110
  330.3 1.2 reshape.82
  331.5 1.3 copy.101
  333.0 6.0 %fusion.61 = bf16[2,128,2,64]{3,2,0,1:T(2,128)(2,1)} fusion(bf16[128,64,256]{2,1,0:T(8,128)(2,1)} %param.16, bf16[2,128,2,64]{3,2,0,1:T(2,128)(2,1)S(1)} %copy.77, f32[256]{0:T(256)S(1)} %copy-done.12), kind=kOutput, calls=%fused_computation.34 | convolution fusion | flops 33849344 | bytes 4326400 | tf_op jit(solution)/shard_map/cmfl,mil->cmfi/dot_general | solution.py:46
  339.2 29.0 %all-reduce.5.cloned.1.call-done = bf16[2,128,2,64]{3,2,0,1:T(2,128)(2,1)} async-done(((bf16[2,128,2,64]{3,2,0,1:T(2,128)(2,1)}), bf16[2,128,2,64]{3,2,0,1:T(2,128)(2,1)}) %all-reduce.5.cloned.1.call-update) | async-done | bytes 65552 | tf_op jit(solution)/shard_map/psum | solution.py:112
  368.2 3.7 constant_dynamic-slice_fusion.8
  371.9 1.5 collective-permute-start.4
  373.4 1.5 collective-permute-start.5
  375.5 2.4 collective-permute-start.7
  377.9 1.4 collective-permute-start.8
  380.0 3.3 collective-permute-start.9
  386.0 1.0 copy.81
  387.1 6.9 %collective-permute-done.7 = bf16[2,128,2,8]{3,2,0,1:T(2,128)(2,1)} collective-permute-done((bf16[2,128,2,8]{3,2,0,1:T(2,128)(2,1)S(1)}, bf16[2,128,2,8]{3,2,0,1:T(2,128)(2,1)}, u32[]{:S(2)}, u32[]{:S(2)}) %collective-permute-start.7) | collective-permute-done | bytes 8224 | tf_op jit(solution)/shard_map/ppermute | solution.py:123
  395.0 2.8 collective-permute-done.8
  398.9 1.0 copy.84
  399.9 1.0 copy.85
  401.1 18.4 %fusion.10 = f32[2,8,10752]{2,1,0:T(8,128)} fusion(bf16[10752,1024]{1,0:T(8,128)(2,1)} %get-tuple-element.64, bf16[10752,1024]{1,0:T(8,128)(2,1)} %get-tuple-element.65, f32[2,8]{1,0:T(2,128)S(1)} %get-tuple-element.63, bf16[2048,16]{0,1:T(8,128)(2,1)S(1)} %bitcast.198), kind=kOutput, calls=%fused_computation.15 | convolution fusion | flops 792895488 | bytes 44793920 | tf_op jit(solution)/shard_map/dot_general | solution.py:53
  419.5 1.4 multiply_multiply_fusion
  420.9 1.3 collective-permute-start.11
  422.2 1.3 collective-permute-start.13
  423.8 3.0 collective-permute-done.11
  426.9 1.9 collective-permute-done.13
  428.9 2.4 fusion.135
  431.3 4.8 collective-permute-start.12
  436.2 2.6 collective-permute-start.14
  439.3 1.8 multiply_bitcast_fusion.1
  441.6 19.4 %fusion.67 = bf16[2,1024,2,8]{1,3,2,0:T(8,128)(2,1)S(1)} fusion(bf16[2,1024,10752,1]{2,1,3,0:T(8,128)(2,1)} %bitcast.180, bf16[1,8,10752]{2,1,0:T(8,128)(2,1)S(1)} %get-tuple-element.14, bf16[1,8,10752]{2,1,0:T(8,128)(2,1)S(1)} %get-tuple-element.12, f32[2,8]{1,0:T(2,128)S(1)} %get-tuple-element.62), kind=kOutput, calls=%fused_computation.38 | convolution fusion | flops 705396736 | bytes 44449856 | tf_op jit(solution)/shard_map/dot_general | solution.py:36
  461.7 1.1 reshape.83
  462.8 12.6 %all_to_all.37 = bf16[8,2,2048]{2,1,0:T(2,128)(2,1)S(1)} all-to-all(bf16[8,2,2048]{2,1,0:T(2,128)(2,1)S(1)} %reshape.83), channel_id=1, replica_groups=mesh['lat'=8,'deg'=4] {'lat'}, dimensions={0} | all-to-all | bytes 131072 | tf_op jit(solution)/shard_map/all_to_all | solution.py:110
  475.4 1.2 reshape.84
  476.6 1.3 copy.103
  478.7 6.1 %fusion.56 = bf16[2,128,2,64]{3,2,0,1:T(2,128)(2,1)} fusion(bf16[128,64,256]{2,1,0:T(8,128)(2,1)} %param.16, bf16[2,128,2,64]{3,2,0,1:T(2,128)(2,1)} %copy.89, f32[256]{0:T(256)S(1)} %copy-done.12), kind=kOutput, calls=%fused_computation.33 | convolution fusion | flops 33849344 | bytes 4326400 | tf_op jit(solution)/shard_map/cmfl,mil->cmfi/dot_general | solution.py:46
  484.9 28.4 %all-reduce.7.cloned.1.call-done = bf16[2,128,2,64]{3,2,0,1:T(2,128)(2,1)} async-done(((bf16[2,128,2,64]{3,2,0,1:T(2,128)(2,1)}), bf16[2,128,2,64]{3,2,0,1:T(2,128)(2,1)}) %all-reduce.7.cloned.1.call-update) | async-done | bytes 65552 | tf_op jit(solution)/shard_map/psum | solution.py:112
  513.3 3.7 constant_dynamic-slice_fusion
  518.0 1.5 collective-permute-start.15
  519.5 1.5 collective-permute-start.16
  521.6 2.4 collective-permute-start.18
  524.0 1.4 collective-permute-start.19
  525.5 3.4 collective-permute-start.20
  531.5 1.0 copy.93
  532.6 7.6 %collective-permute-done.18 = bf16[2,128,2,8]{3,2,0,1:T(2,128)(2,1)} collective-permute-done((bf16[2,128,2,8]{3,2,0,1:T(2,128)(2,1)}, bf16[2,128,2,8]{3,2,0,1:T(2,128)(2,1)}, u32[]{:S(2)}, u32[]{:S(2)}) %collective-permute-start.18) | collective-permute-done | bytes 8224 | tf_op jit(solution)/shard_map/ppermute | solution.py:123
  541.3 2.9 collective-permute-done.19
  545.2 1.0 copy.96
  546.2 1.0 copy.97
  547.4 18.4 %fusion.13 = f32[2,8,10752]{2,1,0:T(8,128)} fusion(bf16[10752,1024]{1,0:T(8,128)(2,1)} %get-tuple-element.64, bf16[10752,1024]{1,0:T(8,128)(2,1)} %get-tuple-element.65, f32[2,8]{1,0:T(2,128)S(1)} %get-tuple-element.63, bf16[2048,16]{0,1:T(8,128)(2,1)S(1)} %bitcast.197), kind=kOutput, calls=%fused_computation.16 | convolution fusion | flops 792895488 | bytes 44793920 | tf_op jit(solution)/shard_map/dot_general | solution.py:53
  565.8 1.9 fusion.68
  567.7 1.3 collective-permute-start.22
  569.0 1.9 pad_maximum_fusion.4
  571.1 2.5 collective-permute-done.22
  573.7 1.4 fusion.126
  575.1 3.2 collective-permute-start.23
  (140 shorter events, 22.2 us)
Async XLA Ops:
  7.2 194.6 %copy-start.2 = (f32[8,10752]{1,0:T(8,128)S(1)}, f32[8,10752]{1,0:T(8,128)}, u32[]{:S(2)}) copy-start(f32[8,10752]{1,0:T(8,128)} %param.9) | copy-start | bytes 1032196
  7.2 361.0 %all-reduce.5.cloned.1.call-start = ((), (), s32[]{:S(2)}) async-start(), calls=%async_computation.2 | async-start | bytes 262144 | tf_op jit(solution)/shard_map/psum | solution.py:112
  8.5 224.1 %collective-permute-start.2 = (bf16[1,10752]{1,0:T(2,128)(2,1)S(1)}, bf16[1,10752]{1,0:T(2,128)(2,1)S(1)}, u32[]{:S(2)}, u32[]{:S(2)}) collective-permute-start(bf16[1,10752]{1,0:T(2,128)(2,1)S(1)} %slice.280), channel_id=1, source_target_pairs={{4,0},{8,4},{12,8},{16,12},{20,16},{24,20},{28,24},{5,1},{9,5},{13... | collective-permute-start | bytes 64520 | tf_op jit(solution)/shard_map/ppermute | solution.py:18
  10.8 221.9 %collective-permute-start.1 = (bf16[1,10752]{1,0:T(2,128)(2,1)S(1)}, bf16[1,10752]{1,0:T(2,128)(2,1)S(1)}, u32[]{:S(2)}, u32[]{:S(2)}) collective-permute-start(bf16[1,10752]{1,0:T(2,128)(2,1)S(1)} %slice.281), channel_id=1, source_target_pairs={{4,0},{8,4},{12,8},{16,12},{20,16},{24,20},{28,24},{5,1},{9,5},{13... | collective-permute-start | bytes 64520 | tf_op jit(solution)/shard_map/ppermute | solution.py:18
  13.2 219.6 %collective-permute-start = (bf16[1,10752]{1,0:T(2,128)(2,1)S(1)}, bf16[1,10752]{1,0:T(2,128)(2,1)S(1)}, u32[]{:S(2)}, u32[]{:S(2)}) collective-permute-start(bf16[1,10752]{1,0:T(2,128)(2,1)S(1)} %slice.282), channel_id=1, source_target_pairs={{4,0},{8,4},{12,8},{16,12},{20,16},{24,20},{28,24},{5,1},{9,5},{13... | collective-permute-start | bytes 64520 | tf_op jit(solution)/shard_map/ppermute | solution.py:18
  202.5 29.9 %copy-start.1 = (f32[8,10752]{1,0:T(8,128)S(1)}, f32[8,10752]{1,0:T(8,128)}, u32[]{:S(2)}) copy-start(f32[8,10752]{1,0:T(8,128)} %param.13) | copy-start | bytes 1032196
  202.5 30.3 %copy-start = (s32[8,10752]{1,0:T(8,128)S(1)}, s32[8,10752]{1,0:T(8,128)}, u32[]{:S(2)}) copy-start(s32[8,10752]{1,0:T(8,128)} %param.15) | copy-start | bytes 1032196
  202.5 30.3 %slice-start = ((f32[8,10752]{1,0:T(8,128)}), f32[8,1]{1,0:T(8,128)S(1)}, s32[]{:S(2)}) async-start(f32[8,10752]{1,0:T(8,128)} %param.13), calls=%async_computation.4 | async-start | bytes 8192 | tf_op jit(solution)/shard_map/jit(_roll_static)/slice | solution.py:87
  235.2 193.6 %copy-start.5 = (f32[8,10752]{1,0:T(8,128)}, f32[8,10752]{1,0:T(8,128)S(1)}, u32[]{:S(2)}) copy-start(f32[8,10752]{1,0:T(8,128)S(1)} %get-tuple-element.34) | copy-start | bytes 1032196
  235.2 58.1 %collective-permute-start.3 = (bf16[1,10752]{1,0:T(2,128)(2,1)S(1)}, bf16[1,10752]{1,0:T(2,128)(2,1)S(1)}, u32[]{:S(2)}, u32[]{:S(2)}) collective-permute-start(bf16[1,10752]{1,0:T(2,128)(2,1)S(1)} %slice.279), channel_id=1, source_target_pairs={{0,4},{4,8},{8,12},{12,16},{16,20},{20,24},{24,28},{1,5},{5,9},{9,... | collective-permute-start | bytes 64520 | tf_op jit(solution)/shard_map/ppermute | solution.py:18
  242.0 52.3 %copy-start.10 = (bf16[1,8,10752]{2,1,0:T(8,128)(2,1)S(1)}, bf16[1,8,10752]{2,1,0:T(8,128)(2,1)}, u32[]{:S(2)}) copy-start(bf16[1,8,10752]{2,1,0:T(8,128)(2,1)} %convert_bitcast_fusion.3) | copy-start | bytes 516100
  293.3 39.7 %copy-start.12 = (f32[256]{0:T(256)S(1)}, f32[256]{0:T(256)}, u32[]{:S(2)}) copy-start(f32[256]{0:T(256)} %param.17) | copy-start | bytes 3076
  333.0 95.9 %copy-start.3 = (f32[8,10752]{1,0:T(8,128)S(1)}, f32[8,10752]{1,0:T(8,128)}, u32[]{:S(2)}) copy-start(f32[8,10752]{1,0:T(8,128)} %param.14) | copy-start | bytes 1032196
  333.0 95.9 %copy-start.7 = (f32[8,10752]{1,0:T(8,128)S(1)}, f32[8,10752]{1,0:T(8,128)}, u32[]{:S(2)}) copy-start(f32[8,10752]{1,0:T(8,128)} %get-tuple-element.35) | copy-start | bytes 1032196
  339.1 174.2 %all-reduce.7.cloned.1.call-start = ((), (), s32[]{:S(2)}) async-start(), calls=%async_computation.3 | async-start | bytes 262144 | tf_op jit(solution)/shard_map/psum | solution.py:112
  371.9 7.4 %collective-permute-start.4 = (bf16[2,128,2,8]{3,2,0,1:T(2,128)(2,1)}, bf16[2,128,2,8]{3,2,0,1:T(2,128)(2,1)S(1)}, u32[]{:S(2)}, u32[]{:S(2)}) collective-permute-start(bf16[2,128,2,8]{3,2,0,1:T(2,128)(2,1)} %get-tuple-element.60), channel_id=1, source_target_pairs={{0,4},{4,0},{8,12},{12,8},{16,20},{20,16},{24,28},{28,24},{1,5},{5... | collective-permute-start | bytes 24584 | tf_op jit(solution)/shard_map/ppermute | solution.py:123
  373.4 11.0 %collective-permute-start.5 = (bf16[2,128,2,8]{3,2,0,1:T(2,128)(2,1)}, bf16[2,128,2,8]{3,2,0,1:T(2,128)(2,1)}, u32[]{:S(2)}, u32[]{:S(2)}) collective-permute-start(bf16[2,128,2,8]{3,2,0,1:T(2,128)(2,1)} %get-tuple-element.59), channel_id=1, source_target_pairs={{0,8},{4,12},{8,0},{12,4},{16,24},{20,28},{24,16},{28,20},{1,9},{5... | collective-permute-start | bytes 24584 | tf_op jit(solution)/shard_map/ppermute | solution.py:123
  374.9 11.1 %collective-permute-start.6 = (bf16[2,128,2,8]{3,2,0,1:T(2,128)(2,1)}, bf16[2,128,2,8]{3,2,0,1:T(2,128)(2,1)}, u32[]{:S(2)}, u32[]{:S(2)}) collective-permute-start(bf16[2,128,2,8]{3,2,0,1:T(2,128)(2,1)} %get-tuple-element.58), channel_id=1, source_target_pairs={{0,12},{4,8},{8,4},{12,0},{16,28},{20,24},{24,20},{28,16},{1,13},{... | collective-permute-start | bytes 24584 | tf_op jit(solution)/shard_map/ppermute | solution.py:123
  375.5 18.5 %collective-permute-start.7 = (bf16[2,128,2,8]{3,2,0,1:T(2,128)(2,1)S(1)}, bf16[2,128,2,8]{3,2,0,1:T(2,128)(2,1)}, u32[]{:S(2)}, u32[]{:S(2)}) collective-permute-start(bf16[2,128,2,8]{3,2,0,1:T(2,128)(2,1)S(1)} %get-tuple-element.57), channel_id=1, source_target_pairs={{0,16},{4,20},{8,24},{12,28},{16,0},{20,4},{24,8},{28,12},{1,17},{... | collective-permute-start | bytes 24584 | tf_op jit(solution)/shard_map/ppermute | solution.py:123
  377.9 19.9 %collective-permute-start.8 = (bf16[2,128,2,8]{3,2,0,1:T(2,128)(2,1)S(1)}, bf16[2,128,2,8]{3,2,0,1:T(2,128)(2,1)}, u32[]{:S(2)}, u32[]{:S(2)}) collective-permute-start(bf16[2,128,2,8]{3,2,0,1:T(2,128)(2,1)S(1)} %get-tuple-element.56), channel_id=1, source_target_pairs={{0,20},{4,16},{8,28},{12,24},{16,4},{20,0},{24,12},{28,8},{1,21},{... | collective-permute-start | bytes 24584 | tf_op jit(solution)/shard_map/ppermute | solution.py:123
  379.4 0.7 copy-start.11
  380.0 18.8 %collective-permute-start.9 = (bf16[2,128,2,8]{3,2,0,1:T(2,128)(2,1)S(1)}, bf16[2,128,2,8]{3,2,0,1:T(2,128)(2,1)}, u32[]{:S(2)}, u32[]{:S(2)}) collective-permute-start(bf16[2,128,2,8]{3,2,0,1:T(2,128)(2,1)S(1)} %get-tuple-element.55), channel_id=1, source_target_pairs={{0,24},{4,28},{8,16},{12,20},{16,8},{20,12},{24,0},{28,4},{1,25},{... | collective-permute-start | bytes 24584 | tf_op jit(solution)/shard_map/ppermute | solution.py:123
  384.4 15.5 %collective-permute-start.10 = (bf16[2,128,2,8]{3,2,0,1:T(2,128)(2,1)S(1)}, bf16[2,128,2,8]{3,2,0,1:T(2,128)(2,1)}, u32[]{:S(2)}, u32[]{:S(2)}) collective-permute-start(bf16[2,128,2,8]{3,2,0,1:T(2,128)(2,1)S(1)} %get-tuple-element.54), channel_id=1, source_target_pairs={{0,28},{4,24},{8,20},{12,16},{16,12},{20,8},{24,4},{28,0},{1,29},{... | collective-permute-start | bytes 24584 | tf_op jit(solution)/shard_map/ppermute | solution.py:123
  420.9 5.9 %collective-permute-start.11 = (bf16[1,10752]{1,0:T(2,128)(2,1)S(1)}, bf16[1,10752]{1,0:T(2,128)(2,1)S(1)}, u32[]{:S(2)}, u32[]{:S(2)}) collective-permute-start(bf16[1,10752]{1,0:T(2,128)(2,1)S(1)} %slice.278), channel_id=1, source_target_pairs={{4,0},{8,4},{12,8},{16,12},{20,16},{24,20},{28,24},{5,1},{9,5},{13... | collective-permute-start | bytes 64520 | tf_op jit(solution)/shard_map/ppermute | solution.py:18
  422.2 6.5 %collective-permute-start.13 = (bf16[1,10752]{1,0:T(2,128)(2,1)S(1)}, bf16[1,10752]{1,0:T(2,128)(2,1)S(1)}, u32[]{:S(2)}, u32[]{:S(2)}) collective-permute-start(bf16[1,10752]{1,0:T(2,128)(2,1)S(1)} %slice.276), channel_id=1, source_target_pairs={{4,0},{8,4},{12,8},{16,12},{20,16},{24,20},{28,24},{5,1},{9,5},{13... | collective-permute-start | bytes 64520 | tf_op jit(solution)/shard_map/ppermute | solution.py:18
  431.3 7.5 %collective-permute-start.12 = (bf16[1,10752]{1,0:T(2,128)(2,1)S(1)}, bf16[1,10752]{1,0:T(2,128)(2,1)S(1)}, u32[]{:S(2)}, u32[]{:S(2)}) collective-permute-start(bf16[1,10752]{1,0:T(2,128)(2,1)S(1)} %slice.277), channel_id=1, source_target_pairs={{0,4},{4,8},{8,12},{12,16},{16,20},{20,24},{24,28},{1,5},{5,9},{9,... | collective-permute-start | bytes 64520 | tf_op jit(solution)/shard_map/ppermute | solution.py:18
  436.2 5.1 collective-permute-start.14
  478.7 90.3 %copy-start.9 = (f32[1,8,10752]{2,1,0:T(8,128)S(1)}, f32[1,8,10752]{2,1,0:T(8,128)}, u32[]{:S(2)}) copy-start(f32[1,8,10752]{2,1,0:T(8,128)} %get-tuple-element.4) | copy-start | bytes 1032196
  478.7 95.0 %copy-start.4 = (f32[8,10752]{1,0:T(8,128)S(1)}, f32[8,10752]{1,0:T(8,128)}, u32[]{:S(2)}) copy-start(f32[8,10752]{1,0:T(8,128)} %param.14) | copy-start | bytes 1032196
  478.7 95.0 %copy-start.6 = (f32[8,10752]{1,0:T(8,128)S(1)}, f32[8,10752]{1,0:T(8,128)}, u32[]{:S(2)}) copy-start(f32[8,10752]{1,0:T(8,128)} %copy-done.5) | copy-start | bytes 1032196
  478.7 95.0 %copy-start.8 = (f32[8,10752]{1,0:T(8,128)S(1)}, f32[8,10752]{1,0:T(8,128)}, u32[]{:S(2)}) copy-start(f32[8,10752]{1,0:T(8,128)} %get-tuple-element.35) | copy-start | bytes 1032196
  518.0 7.4 %collective-permute-start.15 = (bf16[2,128,2,8]{3,2,0,1:T(2,128)(2,1)}, bf16[2,128,2,8]{3,2,0,1:T(2,128)(2,1)}, u32[]{:S(2)}, u32[]{:S(2)}) collective-permute-start(bf16[2,128,2,8]{3,2,0,1:T(2,128)(2,1)} %get-tuple-element.52), channel_id=1, source_target_pairs={{0,4},{4,0},{8,12},{12,8},{16,20},{20,16},{24,28},{28,24},{1,5},{5... | collective-permute-start | bytes 24584 | tf_op jit(solution)/shard_map/ppermute | solution.py:123
  519.5 10.4 %collective-permute-start.16 = (bf16[2,128,2,8]{3,2,0,1:T(2,128)(2,1)}, bf16[2,128,2,8]{3,2,0,1:T(2,128)(2,1)}, u32[]{:S(2)}, u32[]{:S(2)}) collective-permute-start(bf16[2,128,2,8]{3,2,0,1:T(2,128)(2,1)} %get-tuple-element.51), channel_id=1, source_target_pairs={{0,8},{4,12},{8,0},{12,4},{16,24},{20,28},{24,16},{28,20},{1,9},{5... | collective-permute-start | bytes 24584 | tf_op jit(solution)/shard_map/ppermute | solution.py:123
  521.0 10.5 %collective-permute-start.17 = (bf16[2,128,2,8]{3,2,0,1:T(2,128)(2,1)}, bf16[2,128,2,8]{3,2,0,1:T(2,128)(2,1)}, u32[]{:S(2)}, u32[]{:S(2)}) collective-permute-start(bf16[2,128,2,8]{3,2,0,1:T(2,128)(2,1)} %get-tuple-element.50), channel_id=1, source_target_pairs={{0,12},{4,8},{8,4},{12,0},{16,28},{20,24},{24,20},{28,16},{1,13},{... | collective-permute-start | bytes 24584 | tf_op jit(solution)/shard_map/ppermute | solution.py:123
  521.6 18.6 %collective-permute-start.18 = (bf16[2,128,2,8]{3,2,0,1:T(2,128)(2,1)}, bf16[2,128,2,8]{3,2,0,1:T(2,128)(2,1)}, u32[]{:S(2)}, u32[]{:S(2)}) collective-permute-start(bf16[2,128,2,8]{3,2,0,1:T(2,128)(2,1)} %get-tuple-element.49), channel_id=1, source_target_pairs={{0,16},{4,20},{8,24},{12,28},{16,0},{20,4},{24,8},{28,12},{1,17},{... | collective-permute-start | bytes 24584 | tf_op jit(solution)/shard_map/ppermute | solution.py:123
  524.0 20.2 %collective-permute-start.19 = (bf16[2,128,2,8]{3,2,0,1:T(2,128)(2,1)}, bf16[2,128,2,8]{3,2,0,1:T(2,128)(2,1)}, u32[]{:S(2)}, u32[]{:S(2)}) collective-permute-start(bf16[2,128,2,8]{3,2,0,1:T(2,128)(2,1)} %get-tuple-element.48), channel_id=1, source_target_pairs={{0,20},{4,16},{8,28},{12,24},{16,4},{20,0},{24,12},{28,8},{1,21},{... | collective-permute-start | bytes 24584 | tf_op jit(solution)/shard_map/ppermute | solution.py:123
  525.5 19.7 %collective-permute-start.20 = (bf16[2,128,2,8]{3,2,0,1:T(2,128)(2,1)}, bf16[2,128,2,8]{3,2,0,1:T(2,128)(2,1)}, u32[]{:S(2)}, u32[]{:S(2)}) collective-permute-start(bf16[2,128,2,8]{3,2,0,1:T(2,128)(2,1)} %get-tuple-element.47), channel_id=1, source_target_pairs={{0,24},{4,28},{8,16},{12,20},{16,8},{20,12},{24,0},{28,4},{1,25},{... | collective-permute-start | bytes 24584 | tf_op jit(solution)/shard_map/ppermute | solution.py:123
  529.9 16.3 %collective-permute-start.21 = (bf16[2,128,2,8]{3,2,0,1:T(2,128)(2,1)}, bf16[2,128,2,8]{3,2,0,1:T(2,128)(2,1)}, u32[]{:S(2)}, u32[]{:S(2)}) collective-permute-start(bf16[2,128,2,8]{3,2,0,1:T(2,128)(2,1)} %get-tuple-element.46), channel_id=1, source_target_pairs={{0,28},{4,24},{8,20},{12,16},{16,12},{20,8},{24,4},{28,0},{1,29},{... | collective-permute-start | bytes 24584 | tf_op jit(solution)/shard_map/ppermute | solution.py:123
  567.7 5.9 %collective-permute-start.22 = (bf16[1,10752]{1,0:T(2,128)(2,1)S(1)}, bf16[1,10752]{1,0:T(2,128)(2,1)S(1)}, u32[]{:S(2)}, u32[]{:S(2)}) collective-permute-start(bf16[1,10752]{1,0:T(2,128)(2,1)S(1)} %slice.274), channel_id=1, source_target_pairs={{4,0},{8,4},{12,8},{16,12},{20,16},{24,20},{28,24},{5,1},{9,5},{13... | collective-permute-start | bytes 64520 | tf_op jit(solution)/shard_map/ppermute | solution.py:18
  575.1 4.8 collective-permute-start.23
Sparse Core Ops, SparseCore 0:
  339.2 28.9 all-reduce.4
  485.0 28.2 all-reduce.6
